TPU v7x, 32 devices: a whole 2x2x4 slice. The times are simulated.
32 devices in a mesh: groups: 2 (over x), row: 16 (over z, y, core).
Axes of the slice: x: 2, y: 2, z: 4, core: 2. Of those that a mesh axis runs over, the one named last changes fastest.
Arguments:
- hamiltonian: bfloat16 [96, 16, 128, 128], P(('groups', 'row')), parts along dimension 0, may hold values from -0.0625 to 0.0625
- coupling_cols: int32 [96, 16], P(('groups', 'row')), parts along dimension 0, may hold values from 0 to 47, as said below
- pattern_cols: int32 [96, 16], P(('groups', 'row')), parts along dimension 0, may hold values from 0 to 47, as said below
- current_term: bfloat16 [96, 16, 128, 128], P(('groups', 'row')), parts along dimension 0, may hold values from -6 to 6
- previous_term: bfloat16 [96, 16, 128, 128], P(('groups', 'row')), parts along dimension 0, may hold values from -6 to 6
Outputs:
- next_term: bfloat16 [96, 16, 128, 128], P(('groups', 'row')), parts along dimension 0
- after_term: bfloat16 [96, 16, 128, 128], P(('groups', 'row')), parts along dimension 0
There are 2 independent parts, one for each index of `groups`. A program takes and returns all parts, laid end to end along the dimension named above; each array names one. Nothing has to cross between parts.
Inputs may be any that keep to these rules, and one draw needn't show every extreme that they name: `coupling_cols`: block row i holds 16 distinct block columns (i + o) mod 48, o from -8 to 8 in increasing order, i itself always among them. `pattern_cols`: block row i holds 16 distinct block columns (i + o) mod 48, o from -8 to 8 in increasing order, i itself always among them.
All inputs are finite; a program needn't handle non-finite values.
Results may differ from a plain program's by a relative error of at most 0.004.
Values may be sent and summed in bfloat16 or wider, within the bound.
A program may use at most 128 MiB of HBM per device.

v0:
```python
import jax
import jax.numpy as jnp
from jax import lax
from jax.sharding import PartitionSpec as P

REACH = 8


def passed_along(value, axis, steps):
    count = lax.axis_size(axis)
    pairs = [(source, (source + steps) % count) for source in range(count)]
    return lax.ppermute(value, axis, pairs)


def extended_rows(term_rows, pattern_rows):
    local_rows = term_rows.shape[0]
    distance_max = (REACH + local_rows - 1) // local_rows
    below_vals = []
    below_cols = []
    above_vals = []
    above_cols = []
    for distance in range(1, distance_max + 1):
        needed = min(local_rows, REACH - (distance - 1) * local_rows)
        arrived = passed_along((term_rows, pattern_rows), "row", distance)
        below_vals.insert(0, arrived[0][local_rows - needed :])
        below_cols.insert(0, arrived[1][local_rows - needed :])
        arrived = passed_along((term_rows, pattern_rows), "row", -distance)
        above_vals.append(arrived[0][:needed])
        above_cols.append(arrived[1][:needed])
    values = jnp.concatenate(below_vals + [term_rows] + above_vals, axis=0)
    columns = jnp.concatenate(below_cols + [pattern_rows] + above_cols, axis=0)
    return (values, columns)


def advance(hamiltonian, coupling_cols, pattern_cols, current_term, previous_term):
    local_rows = current_term.shape[0]
    order_rows = local_rows * lax.axis_size("row")
    first_row = lax.axis_index("row") * local_rows - REACH
    values, columns = extended_rows(current_term, pattern_cols)
    positions = (coupling_cols - first_row) % order_rows

    def advance_row(inputs):
        blocks, neighbours, own_cols, earlier = inputs
        picked = jnp.take(values, neighbours, axis=0)
        picked_cols = jnp.take(columns, neighbours, axis=0)
        matches = (own_cols[None, :, None] == picked_cols[:, None, :]).astype(jnp.bfloat16)
        chosen = jnp.einsum(
            "kmn,knab->kmab", matches, picked, preferred_element_type=jnp.float32
        ).astype(jnp.bfloat16)
        product = jnp.einsum("kac,kmcb->mab", blocks, chosen, preferred_element_type=jnp.float32)
        return (2.0 * product - earlier.astype(jnp.float32)).astype(jnp.bfloat16)

    return lax.map(advance_row, (hamiltonian, positions, pattern_cols, previous_term))


def body(hamiltonian, coupling_cols, pattern_cols, current_term, previous_term):
    next_term = advance(hamiltonian, coupling_cols, pattern_cols, current_term, previous_term)
    after_term = advance(hamiltonian, coupling_cols, pattern_cols, next_term, current_term)
    return (next_term, after_term)


def solution(mesh):
    placed = (
        P(("groups", "row"), None, None, None),
        P(("groups", "row"), None),
        P(("groups", "row"), None),
        P(("groups", "row"), None, None, None),
        P(("groups", "row"), None, None, None),
    )
    return jax.shard_map(
        body,
        mesh=mesh,
        in_specs=placed,
        out_specs=(P(("groups", "row"), None, None, None), P(("groups", "row"), None, None, None)),
        check_vma=False,
    )
```

profile of v0, /device:TPU:0, one launch (start us, length us, event | category | flops | bytes accessed | tf_op | source)
XLA Modules:
  0.0 629.1 jit_solution(12820383249968583690)
XLA Ops:
  9.1 78.4 %collective-permute-done = s32[3,16]{1,0:T(4,128)S(1)} collective-permute-done((s32[3,16]{1,0:T(4,128)}, s32[3,16]{1,0:T(4,128)S(1)}, u32[]{:S(2)}, u32[]{:S(2)}) %collective-permute-start) | collective-permute-done | bytes 224 | tf_op jit(solution)/shard_map/ppermute | solution.py:12
  101.9 5.9 collective-permute-done.2
  124.0 26.0 %collective-permute-done.10 = bf16[3,16,128,128]{3,2,1,0:T(8,128)(2,1)} collective-permute-done((bf16[3,16,128,128]{3,2,1,0:T(8,128)(2,1)}, bf16[3,16,128,128]{3,2,1,0:T(8,128)(2,1)}, u32[]{:S(2)}, u32[]{:S(2)}) %collective-permute-start.10) | collective-permute-done | bytes 1572896 | tf_op jit(solution)/shard_map/ppermute | solution.py:12
  151.8 30.1 %collective-permute-done.11 = bf16[3,16,128,128]{3,2,1,0:T(8,128)(2,1)} collective-permute-done((bf16[3,16,128,128]{3,2,1,0:T(8,128)(2,1)}, bf16[3,16,128,128]{3,2,1,0:T(8,128)(2,1)}, u32[]{:S(2)}, u32[]{:S(2)}) %collective-permute-start.11) | collective-permute-done | bytes 1572896 | tf_op jit(solution)/shard_map/ppermute | solution.py:12
  187.1 147.7 %while.20 = (s32[]{:T(128)}, bf16[3,16,128,128]{3,2,1,0:T(8,128)(2,1)S(1)}, s32[3,16]{1,0:T(4,128)S(1)}, s32[3,16]{1,0:T(4,128)S(1)}, s32[19,16]{1,0:T(8,128)S(1...) while((s32[]{:T(128)}, ...), condition=%wide.region_1.4_spmd, body=%wide.region_0.3_spmd.sunk | while | flops 1213207936 | bytes 81275024 | solution.py:53
  187.2 8.7 %gather_fusion = bf16[16,16,128,128]{3,2,1,0:T(8,128)(2,1)} fusion(bf16[19,16,128,128]{3,2,1,0:T(8,128)(2,1)} %get-tuple-element.273, s32[1024]{0:T(1024)S(1)} %pad_clamp_fusion.4), kind=kCustom, calls=%fused_computation.1.clone.clone.1 | custom fusion | bytes 16777280 | tf_op jit(solution)/shard_map/while/body/eval_jaxpr/jit(_take)/gather | solution.py:44
  195.9 7.6 %broadcast_select_fusion.8 = bf16[16,16,128,128]{3,2,1,0:T(8,128)(2,1)} fusion(bf16[16,16,128,128]{3,2,1,0:T(8,128)(2,1)} %gather_fusion, pred[16]{0:T(512)(128)(4,1)S(1)} %get-tuple-element.239), kind=kLoop, calls=%fused_computation.8.clone.1 | loop fusion | flops 4194304 | bytes 16777232 | tf_op jit(solution)/shard_map/while/body/eval_jaxpr/jit(_take)/select_n | solution.py:44
  204.1 12.2 %fusion.83 = bf16[16,16,128,128]{3,1,2,0:T(8,128)(2,1)} fusion(bf16[16,16,128,128]{3,2,1,0:T(8,128)(2,1)} %broadcast_select_fusion.8, s32[16,16]{1,0:T(8,128)S(1)} %broadcast_select_fusion.9, s32[16]{0:T(128)S(1)} %fusion.82), kind=kOutput, calls=%fused_computation.4.clone.1 | convolution fusion | flops 134221824 | bytes 16778304 | tf_op jit(solution)/shard_map/while/body/eval_jaxpr/kmn,knab->kmab/dot_general | solution.py:47
  216.3 12.5 %copy.45 = bf16[16,16,128,128]{2,3,0,1:T(8,128)(2,1)} copy(bf16[16,16,128,128]{3,1,2,0:T(8,128)(2,1)} %fusion.83) | data formatting | bytes 16777216 | tf_op jit(solution)/shard_map/while/body/eval_jaxpr/kmn,knab->kmab/dot_general | solution.py:47
  236.4 8.7 %gather_fusion = bf16[16,16,128,128]{3,2,1,0:T(8,128)(2,1)} fusion(bf16[19,16,128,128]{3,2,1,0:T(8,128)(2,1)} %get-tuple-element.273, s32[1024]{0:T(1024)S(1)} %pad_clamp_fusion.4), kind=kCustom, calls=%fused_computation.1.clone.clone.1 | custom fusion | bytes 16777280 | tf_op jit(solution)/shard_map/while/body/eval_jaxpr/jit(_take)/gather | solution.py:44
  245.1 7.6 %broadcast_select_fusion.8 = bf16[16,16,128,128]{3,2,1,0:T(8,128)(2,1)} fusion(bf16[16,16,128,128]{3,2,1,0:T(8,128)(2,1)} %gather_fusion, pred[16]{0:T(512)(128)(4,1)S(1)} %get-tuple-element.239), kind=kLoop, calls=%fused_computation.8.clone.1 | loop fusion | flops 4194304 | bytes 16777232 | tf_op jit(solution)/shard_map/while/body/eval_jaxpr/jit(_take)/select_n | solution.py:44
  253.4 12.2 %fusion.83 = bf16[16,16,128,128]{3,1,2,0:T(8,128)(2,1)} fusion(bf16[16,16,128,128]{3,2,1,0:T(8,128)(2,1)} %broadcast_select_fusion.8, s32[16,16]{1,0:T(8,128)S(1)} %broadcast_select_fusion.9, s32[16]{0:T(128)S(1)} %fusion.82), kind=kOutput, calls=%fused_computation.4.clone.1 | convolution fusion | flops 134221824 | bytes 16778304 | tf_op jit(solution)/shard_map/while/body/eval_jaxpr/kmn,knab->kmab/dot_general | solution.py:47
  265.6 12.5 %copy.45 = bf16[16,16,128,128]{2,3,0,1:T(8,128)(2,1)} copy(bf16[16,16,128,128]{3,1,2,0:T(8,128)(2,1)} %fusion.83) | data formatting | bytes 16777216 | tf_op jit(solution)/shard_map/while/body/eval_jaxpr/kmn,knab->kmab/dot_general | solution.py:47
  285.7 8.7 %gather_fusion = bf16[16,16,128,128]{3,2,1,0:T(8,128)(2,1)} fusion(bf16[19,16,128,128]{3,2,1,0:T(8,128)(2,1)} %get-tuple-element.273, s32[1024]{0:T(1024)S(1)} %pad_clamp_fusion.4), kind=kCustom, calls=%fused_computation.1.clone.clone.1 | custom fusion | bytes 16777280 | tf_op jit(solution)/shard_map/while/body/eval_jaxpr/jit(_take)/gather | solution.py:44
  294.4 7.6 %broadcast_select_fusion.8 = bf16[16,16,128,128]{3,2,1,0:T(8,128)(2,1)} fusion(bf16[16,16,128,128]{3,2,1,0:T(8,128)(2,1)} %gather_fusion, pred[16]{0:T(512)(128)(4,1)S(1)} %get-tuple-element.239), kind=kLoop, calls=%fused_computation.8.clone.1 | loop fusion | flops 4194304 | bytes 16777232 | tf_op jit(solution)/shard_map/while/body/eval_jaxpr/jit(_take)/select_n | solution.py:44
  302.6 12.2 %fusion.83 = bf16[16,16,128,128]{3,1,2,0:T(8,128)(2,1)} fusion(bf16[16,16,128,128]{3,2,1,0:T(8,128)(2,1)} %broadcast_select_fusion.8, s32[16,16]{1,0:T(8,128)S(1)} %broadcast_select_fusion.9, s32[16]{0:T(128)S(1)} %fusion.82), kind=kOutput, calls=%fused_computation.4.clone.1 | convolution fusion | flops 134221824 | bytes 16778304 | tf_op jit(solution)/shard_map/while/body/eval_jaxpr/kmn,knab->kmab/dot_general | solution.py:47
  314.8 12.5 %copy.45 = bf16[16,16,128,128]{2,3,0,1:T(8,128)(2,1)} copy(bf16[16,16,128,128]{3,1,2,0:T(8,128)(2,1)} %fusion.83) | data formatting | bytes 16777216 | tf_op jit(solution)/shard_map/while/body/eval_jaxpr/kmn,knab->kmab/dot_general | solution.py:47
  344.9 90.7 %collective-permute-done.12 = bf16[3,16,128,128]{3,2,1,0:T(8,128)(2,1)S(1)} collective-permute-done((bf16[3,16,128,128]{3,2,1,0:T(8,128)(2,1)S(1)}, bf16[3,16,128,128]{3,2,1,0:T(8,128)(2,1)S(1)}, u32[]{:S(2)}, u32[]{:S(2)}) %collective-permute-start.12) | collective-permute-done | bytes 1572896 | tf_op jit(solution)/shard_map/ppermute | solution.py:12
  435.7 33.6 %collective-permute-done.13 = bf16[3,16,128,128]{3,2,1,0:T(8,128)(2,1)S(1)} collective-permute-done((bf16[3,16,128,128]{3,2,1,0:T(8,128)(2,1)S(1)}, bf16[3,16,128,128]{3,2,1,0:T(8,128)(2,1)S(1)}, u32[]{:S(2)}, u32[]{:S(2)}) %collective-permute-start.13) | collective-permute-done | bytes 1572896 | tf_op jit(solution)/shard_map/ppermute | solution.py:12
  480.2 147.7 %while.21 = (s32[]{:T(128)}, bf16[3,16,128,128]{3,2,1,0:T(8,128)(2,1)S(1)}, s32[3,16]{1,0:T(4,128)S(1)}, s32[3,16]{1,0:T(4,128)S(1)}, s32[19,16]{1,0:T(8,128)S(1...) while((s32[]{:T(128)}, ...), condition=%wide.region_3.6_spmd, body=%wide.region_2.5_spmd.sunk | while | flops 1213207936 | bytes 81275024 | solution.py:53
  480.3 8.7 %gather_fusion.2 = bf16[16,16,128,128]{3,2,1,0:T(8,128)(2,1)} fusion(bf16[19,16,128,128]{3,2,1,0:T(8,128)(2,1)} %get-tuple-element.300, s32[1024]{0:T(1024)S(1)} %pad_clamp_fusion.5), kind=kCustom, calls=%fused_computation.3.clone.clone.1 | custom fusion | bytes 16777280 | tf_op jit(solution)/shard_map/while/body/eval_jaxpr/jit(_take)/gather | solution.py:44
  489.0 7.6 %broadcast_select_fusion.10 = bf16[16,16,128,128]{3,2,1,0:T(8,128)(2,1)} fusion(bf16[16,16,128,128]{3,2,1,0:T(8,128)(2,1)} %gather_fusion.2, pred[16]{0:T(512)(128)(4,1)S(1)} %get-tuple-element.249), kind=kLoop, calls=%fused_computation.36.clone.1 | loop fusion | flops 4194304 | bytes 16777232 | tf_op jit(solution)/shard_map/while/body/eval_jaxpr/jit(_take)/select_n | solution.py:44
  497.2 12.2 %fusion.90 = bf16[16,16,128,128]{3,1,2,0:T(8,128)(2,1)} fusion(bf16[16,16,128,128]{3,2,1,0:T(8,128)(2,1)} %broadcast_select_fusion.10, s32[16,16]{1,0:T(8,128)S(1)} %broadcast_select_fusion.11, s32[16]{0:T(128)S(1)} %fusion.89), kind=kOutput, calls=%fused_computation.32.clone.1 | convolution fusion | flops 134221824 | bytes 16778304 | tf_op jit(solution)/shard_map/while/body/eval_jaxpr/kmn,knab->kmab/dot_general | solution.py:47
  509.4 12.5 %copy.49 = bf16[16,16,128,128]{2,3,0,1:T(8,128)(2,1)} copy(bf16[16,16,128,128]{3,1,2,0:T(8,128)(2,1)} %fusion.90) | data formatting | bytes 16777216 | tf_op jit(solution)/shard_map/while/body/eval_jaxpr/kmn,knab->kmab/dot_general | solution.py:47
  529.5 8.7 %gather_fusion.2 = bf16[16,16,128,128]{3,2,1,0:T(8,128)(2,1)} fusion(bf16[19,16,128,128]{3,2,1,0:T(8,128)(2,1)} %get-tuple-element.300, s32[1024]{0:T(1024)S(1)} %pad_clamp_fusion.5), kind=kCustom, calls=%fused_computation.3.clone.clone.1 | custom fusion | bytes 16777280 | tf_op jit(solution)/shard_map/while/body/eval_jaxpr/jit(_take)/gather | solution.py:44
  538.3 7.6 %broadcast_select_fusion.10 = bf16[16,16,128,128]{3,2,1,0:T(8,128)(2,1)} fusion(bf16[16,16,128,128]{3,2,1,0:T(8,128)(2,1)} %gather_fusion.2, pred[16]{0:T(512)(128)(4,1)S(1)} %get-tuple-element.249), kind=kLoop, calls=%fused_computation.36.clone.1 | loop fusion | flops 4194304 | bytes 16777232 | tf_op jit(solution)/shard_map/while/body/eval_jaxpr/jit(_take)/select_n | solution.py:44
  546.5 12.2 %fusion.90 = bf16[16,16,128,128]{3,1,2,0:T(8,128)(2,1)} fusion(bf16[16,16,128,128]{3,2,1,0:T(8,128)(2,1)} %broadcast_select_fusion.10, s32[16,16]{1,0:T(8,128)S(1)} %broadcast_select_fusion.11, s32[16]{0:T(128)S(1)} %fusion.89), kind=kOutput, calls=%fused_computation.32.clone.1 | convolution fusion | flops 134221824 | bytes 16778304 | tf_op jit(solution)/shard_map/while/body/eval_jaxpr/kmn,knab->kmab/dot_general | solution.py:47
  558.7 12.5 %copy.49 = bf16[16,16,128,128]{2,3,0,1:T(8,128)(2,1)} copy(bf16[16,16,128,128]{3,1,2,0:T(8,128)(2,1)} %fusion.90) | data formatting | bytes 16777216 | tf_op jit(solution)/shard_map/while/body/eval_jaxpr/kmn,knab->kmab/dot_general | solution.py:47
  578.8 8.7 %gather_fusion.2 = bf16[16,16,128,128]{3,2,1,0:T(8,128)(2,1)} fusion(bf16[19,16,128,128]{3,2,1,0:T(8,128)(2,1)} %get-tuple-element.300, s32[1024]{0:T(1024)S(1)} %pad_clamp_fusion.5), kind=kCustom, calls=%fused_computation.3.clone.clone.1 | custom fusion | bytes 16777280 | tf_op jit(solution)/shard_map/while/body/eval_jaxpr/jit(_take)/gather | solution.py:44
  587.5 7.6 %broadcast_select_fusion.10 = bf16[16,16,128,128]{3,2,1,0:T(8,128)(2,1)} fusion(bf16[16,16,128,128]{3,2,1,0:T(8,128)(2,1)} %gather_fusion.2, pred[16]{0:T(512)(128)(4,1)S(1)} %get-tuple-element.249), kind=kLoop, calls=%fused_computation.36.clone.1 | loop fusion | flops 4194304 | bytes 16777232 | tf_op jit(solution)/shard_map/while/body/eval_jaxpr/jit(_take)/select_n | solution.py:44
  595.7 12.2 %fusion.90 = bf16[16,16,128,128]{3,1,2,0:T(8,128)(2,1)} fusion(bf16[16,16,128,128]{3,2,1,0:T(8,128)(2,1)} %broadcast_select_fusion.10, s32[16,16]{1,0:T(8,128)S(1)} %broadcast_select_fusion.11, s32[16]{0:T(128)S(1)} %fusion.89), kind=kOutput, calls=%fused_computation.32.clone.1 | convolution fusion | flops 134221824 | bytes 16778304 | tf_op jit(solution)/shard_map/while/body/eval_jaxpr/kmn,knab->kmab/dot_general | solution.py:47
  608.0 12.5 %copy.49 = bf16[16,16,128,128]{2,3,0,1:T(8,128)(2,1)} copy(bf16[16,16,128,128]{3,1,2,0:T(8,128)(2,1)} %fusion.90) | data formatting | bytes 16777216 | tf_op jit(solution)/shard_map/while/body/eval_jaxpr/kmn,knab->kmab/dot_general | solution.py:47
  (122 shorter events, 117.2 us)
Async XLA Ops:
  0.6 121.4 %copy-start.2 = (bf16[3,16,128,128]{3,2,1,0:T(8,128)(2,1)S(1)}, bf16[3,16,128,128]{3,2,1,0:T(8,128)(2,1)}, u32[]{:S(2)}) copy-start(bf16[3,16,128,128]{3,2,1,0:T(8,128)(2,1)} %param.16) | copy-start | bytes 4718596
  0.6 115.2 %collective-permute-start.6 = (bf16[3,16,128,128]{3,2,1,0:T(8,128)(2,1)}, bf16[3,16,128,128]{3,2,1,0:T(8,128)(2,1)}, u32[]{:S(2)}, u32[]{:S(2)}) collective-permute-start(bf16[3,16,128,128]{3,2,1,0:T(8,128)(2,1)} %param.16), channel_id=1, source_target_pairs={{0,3},{1,4},{2,5},{3,6},{4,7},{5,8},{6,9},{7,10},{8,11},{9,12},{10... | collective-permute-start | bytes 4718600 | tf_op jit(solution)/shard_map/ppermute | solution.py:12
  3.1 115.5 %collective-permute-start.7 = (bf16[3,16,128,128]{3,2,1,0:T(8,128)(2,1)}, bf16[3,16,128,128]{3,2,1,0:T(8,128)(2,1)}, u32[]{:S(2)}, u32[]{:S(2)}) collective-permute-start(bf16[3,16,128,128]{3,2,1,0:T(8,128)(2,1)} %param.16), channel_id=1, source_target_pairs={{0,2},{1,3},{2,4},{3,5},{4,6},{5,7},{6,8},{7,9},{8,10},{9,11},{10,... | collective-permute-start | bytes 4718600 | tf_op jit(solution)/shard_map/ppermute | solution.py:12
  4.6 115.7 %collective-permute-start.8 = (bf16[3,16,128,128]{3,2,1,0:T(8,128)(2,1)}, bf16[3,16,128,128]{3,2,1,0:T(8,128)(2,1)}, u32[]{:S(2)}, u32[]{:S(2)}) collective-permute-start(bf16[3,16,128,128]{3,2,1,0:T(8,128)(2,1)} %param.16), channel_id=1, source_target_pairs={{0,1},{1,2},{2,3},{3,4},{4,5},{5,6},{6,7},{7,8},{8,9},{9,10},{10,1... | collective-permute-start | bytes 4718600 | tf_op jit(solution)/shard_map/ppermute | solution.py:12
  5.1 117.3 %collective-permute-start.9 = (bf16[3,16,128,128]{3,2,1,0:T(8,128)(2,1)}, bf16[3,16,128,128]{3,2,1,0:T(8,128)(2,1)}, u32[]{:S(2)}, u32[]{:S(2)}) collective-permute-start(bf16[3,16,128,128]{3,2,1,0:T(8,128)(2,1)} %param.16), channel_id=1, source_target_pairs={{0,15},{1,0},{2,1},{3,2},{4,3},{5,4},{6,5},{7,6},{8,7},{9,8},{10,9... | collective-permute-start | bytes 4718600 | tf_op jit(solution)/shard_map/ppermute | solution.py:12
  9.1 78.4 %collective-permute-start = (s32[3,16]{1,0:T(4,128)}, s32[3,16]{1,0:T(4,128)S(1)}, u32[]{:S(2)}, u32[]{:S(2)}) collective-permute-start(s32[3,16]{1,0:T(4,128)} %param.15), channel_id=1, source_target_pairs={{0,3},{1,4},{2,5},{3,6},{4,7},{5,8},{6,9},{7,10},{8,11},{9,12},{10... | collective-permute-start | bytes 584 | tf_op jit(solution)/shard_map/ppermute | solution.py:12
  87.4 5.1 collective-permute-start.5
  92.6 9.3 %collective-permute-start.1 = (s32[3,16]{1,0:T(4,128)}, s32[3,16]{1,0:T(4,128)S(1)}, u32[]{:S(2)}, u32[]{:S(2)}) collective-permute-start(s32[3,16]{1,0:T(4,128)} %param.15), channel_id=1, source_target_pairs={{0,2},{1,3},{2,4},{3,5},{4,6},{5,7},{6,8},{7,9},{8,10},{9,11},{10,... | collective-permute-start | bytes 584 | tf_op jit(solution)/shard_map/ppermute | solution.py:12
  101.9 5.9 collective-permute-start.2
  107.8 1.5 collective-permute-start.3
  109.3 3.8 collective-permute-start.4
  113.1 36.9 %collective-permute-start.10 = (bf16[3,16,128,128]{3,2,1,0:T(8,128)(2,1)}, bf16[3,16,128,128]{3,2,1,0:T(8,128)(2,1)}, u32[]{:S(2)}, u32[]{:S(2)}) collective-permute-start(bf16[3,16,128,128]{3,2,1,0:T(8,128)(2,1)} %param.16), channel_id=1, source_target_pairs={{0,14},{1,15},{2,0},{3,1},{4,2},{5,3},{6,4},{7,5},{8,6},{9,7},{10,... | collective-permute-start | bytes 4718600 | tf_op jit(solution)/shard_map/ppermute | solution.py:12
  115.8 66.1 %collective-permute-start.11 = (bf16[3,16,128,128]{3,2,1,0:T(8,128)(2,1)}, bf16[3,16,128,128]{3,2,1,0:T(8,128)(2,1)}, u32[]{:S(2)}, u32[]{:S(2)}) collective-permute-start(bf16[3,16,128,128]{3,2,1,0:T(8,128)(2,1)} %param.16), channel_id=1, source_target_pairs={{0,13},{1,14},{2,15},{3,0},{4,1},{5,2},{6,3},{7,4},{8,5},{9,6},{10... | collective-permute-start | bytes 4718600 | tf_op jit(solution)/shard_map/ppermute | solution.py:12
  120.3 66.8 %copy-start.5 = (s32[3,16]{1,0:T(4,128)S(1)}, s32[3,16]{1,0:T(4,128)}, u32[]{:S(2)}) copy-start(s32[3,16]{1,0:T(4,128)} %param.15) | copy-start | bytes 580
  183.3 3.8 copy-start
  334.9 141.4 %copy-start.3 = (bf16[3,16,128,128]{3,2,1,0:T(8,128)(2,1)}, bf16[3,16,128,128]{3,2,1,0:T(8,128)(2,1)S(1)}, u32[]{:S(2)}) copy-start(bf16[3,16,128,128]{3,2,1,0:T(8,128)(2,1)S(1)} %get-tuple-element.106) | copy-start | bytes 4718596
  334.9 100.7 %collective-permute-start.12 = (bf16[3,16,128,128]{3,2,1,0:T(8,128)(2,1)S(1)}, bf16[3,16,128,128]{3,2,1,0:T(8,128)(2,1)S(1)}, u32[]{:S(2)}, u32[]{:S(2)}) collective-permute-start(bf16[3,16,128,128]{3,2,1,0:T(8,128)(2,1)S(1)} %get-tuple-element.106), channel_id=1, source_target_pairs={{0,3},{1,4},{2,5},{3,6},{4,7},{5,8},{6,9},{7,10},{8,11},{9,12},{10... | collective-permute-start | bytes 4718600 | tf_op jit(solution)/shard_map/ppermute | solution.py:12
  335.1 134.1 %collective-permute-start.13 = (bf16[3,16,128,128]{3,2,1,0:T(8,128)(2,1)S(1)}, bf16[3,16,128,128]{3,2,1,0:T(8,128)(2,1)S(1)}, u32[]{:S(2)}, u32[]{:S(2)}) collective-permute-start(bf16[3,16,128,128]{3,2,1,0:T(8,128)(2,1)S(1)} %get-tuple-element.106), channel_id=1, source_target_pairs={{0,2},{1,3},{2,4},{3,5},{4,6},{5,7},{6,8},{7,9},{8,10},{9,11},{10,... | collective-permute-start | bytes 4718600 | tf_op jit(solution)/shard_map/ppermute | solution.py:12
  335.2 134.3 %collective-permute-start.14 = (bf16[3,16,128,128]{3,2,1,0:T(8,128)(2,1)S(1)}, bf16[3,16,128,128]{3,2,1,0:T(8,128)(2,1)S(1)}, u32[]{:S(2)}, u32[]{:S(2)}) collective-permute-start(bf16[3,16,128,128]{3,2,1,0:T(8,128)(2,1)S(1)} %get-tuple-element.106), channel_id=1, source_target_pairs={{0,1},{1,2},{2,3},{3,4},{4,5},{5,6},{6,7},{7,8},{8,9},{9,10},{10,1... | collective-permute-start | bytes 4718600 | tf_op jit(solution)/shard_map/ppermute | solution.py:12
  338.1 131.9 %collective-permute-start.15 = (bf16[3,16,128,128]{3,2,1,0:T(8,128)(2,1)S(1)}, bf16[3,16,128,128]{3,2,1,0:T(8,128)(2,1)S(1)}, u32[]{:S(2)}, u32[]{:S(2)}) collective-permute-start(bf16[3,16,128,128]{3,2,1,0:T(8,128)(2,1)S(1)} %get-tuple-element.106), channel_id=1, source_target_pairs={{0,15},{1,0},{2,1},{3,2},{4,3},{5,4},{6,5},{7,6},{8,7},{9,8},{10,9... | collective-permute-start | bytes 4718600 | tf_op jit(solution)/shard_map/ppermute | solution.py:12
  342.1 133.9 %collective-permute-start.16 = (bf16[3,16,128,128]{3,2,1,0:T(8,128)(2,1)S(1)}, bf16[3,16,128,128]{3,2,1,0:T(8,128)(2,1)S(1)}, u32[]{:S(2)}, u32[]{:S(2)}) collective-permute-start(bf16[3,16,128,128]{3,2,1,0:T(8,128)(2,1)S(1)} %get-tuple-element.106), channel_id=1, source_target_pairs={{0,14},{1,15},{2,0},{3,1},{4,2},{5,3},{6,4},{7,5},{8,6},{9,7},{10,... | collective-permute-start | bytes 4718600 | tf_op jit(solution)/shard_map/ppermute | solution.py:12
  435.6 40.7 %collective-permute-start.17 = (bf16[3,16,128,128]{3,2,1,0:T(8,128)(2,1)S(1)}, bf16[3,16,128,128]{3,2,1,0:T(8,128)(2,1)S(1)}, u32[]{:S(2)}, u32[]{:S(2)}) collective-permute-start(bf16[3,16,128,128]{3,2,1,0:T(8,128)(2,1)S(1)} %get-tuple-element.106), channel_id=1, source_target_pairs={{0,13},{1,14},{2,15},{3,0},{4,1},{5,2},{6,3},{7,4},{8,5},{9,6},{10... | collective-permute-start | bytes 4718600 | tf_op jit(solution)/shard_map/ppermute | solution.py:12
  476.4 3.8 copy-start.1
  628.0 1.1 copy-start.4
where the time goes:
time: 632 us; the launch traced here: 629 us
  waiting for transfers between devices  286 us (45%)
  local copies, waits for them, and re-layouts  161 us (25%)
  matrix products  108 us (17%)
  other arithmetic  46.8 us (7%)
  starting transfers between devices  25.7 us (4%)
    ppermute x18, waiting for transfers between devices, passed_along(): return lax.ppermute(value, axis, pairs)  286 us
    dot_general x6, local copies, waits for them, and re-layouts, advance_row(): jnp.einsum('kmn,knab->kmab', matches, picked, preferred_element_type=jnp....  74.8 us
    dot_general x6, matrix products, advance_row(): jnp.einsum('kmn,knab->kmab', matches, picked, preferred_element_type=jnp....  73.3 us
    gather x6, local copies, waits for them, and re-layouts, advance_row(): picked = jnp.take(values, neighbours, axis=0)  52.3 us
    select_n x6, other arithmetic, advance_row(): picked = jnp.take(values, neighbours, axis=0)  45.5 us
    dot_general x6, matrix products, advance_row(): jnp.einsum('kac,kmcb->mab', blocks, chosen, preferred_element_type=jnp.fl...  34.9 us
    ppermute x18, starting transfers between devices, passed_along(): return lax.ppermute(value, axis, pairs)  25.7 us
    unnamed x24, local copies, waits for them, and re-layouts  17.5 us
  transfers between devices with their start and end apart: 18, of which 11 were waited for; matrix products, arithmetic and copies ran while one was open for 2% of the time, Pallas kernels for 0%

commit v1 on v0

v1 whole, which is shorter than its diff:
```python
import functools

import jax
import jax.numpy as jnp
from jax import lax
from jax.experimental import pallas as pl
from jax.experimental.pallas import tpu as pltpu
from jax.sharding import PartitionSpec as P

REACH = 8
BAND = 2 * REACH + 1


def exchanges(rows):
    window = rows + 2 * REACH
    plan = []
    for away in range(1, (REACH + rows - 1) // rows + 1):
        shift = away * rows
        for j in range(rows):
            distance = shift - j
            if distance <= REACH:
                plan.append((away, j, REACH + j - shift, shift, 0, BAND - distance))
            distance = shift + j - (rows - 1)
            if distance <= REACH:
                plan.append((-away, j, REACH + j + shift, j, j + shift, window - shift - j))
    return plan


def kernel(count, h_ref, coup_ref, patt_ref, cur_ref, prev_ref, next_ref, after_ref,
           hd, acc, win1, win2, send_sem, recv_sem):
    rows, slots, bs, _ = cur_ref.shape
    order = rows * count
    window = rows + 2 * REACH
    padded = window + window % 2
    plan = exchanges(rows)
    me = lax.axis_index("row")
    peers = sorted({entry[0] for entry in plan})

    def device(away):
        return {"row": lax.rem(me + (away + count), count)}

    barrier = pltpu.get_barrier_semaphore()
    for away in peers:
        pl.semaphore_signal(barrier, inc=1, device_id=device(away),
                            device_id_type=pl.DeviceIdType.MESH)

    def gap(ref, j):
        first = me * rows + (j - REACH - order)
        kept = jnp.int32(0)
        for m in range(slots):
            place = lax.rem(ref[j, m] - first, order)
            kept = kept + jnp.where(place == m, 1, 0).astype(jnp.int32)
        return kept

    def cols(c, n=1):
        return pl.ds(pl.multiple_of(c * bs, bs), n * bs)

    def spread(ref, j, o, d):
        same = jnp.where(o < d, 1.0, 0.0)
        past = jnp.where(o > d, 1.0, 0.0)
        return (ref[j, jnp.minimum(o, slots - 1)].astype(jnp.float32) * same
                + ref[j, jnp.maximum(o - 1, 0)].astype(jnp.float32) * past)

    def packed(ref, lead, j, m, d):
        same = jnp.where(m < d, 1.0, 0.0)
        return (ref[(*lead, cols(j + m))].astype(jnp.float32) * same
                + ref[(*lead, cols(j + m + 1))].astype(jnp.float32) * (1.0 - same))

    patt_gap = [gap(patt_ref, j) for j in range(rows)]
    coup_gap = [gap(coup_ref, j) for j in range(rows)]

    def copies(win, step, j):
        made = []
        for at, (away, row, there, first, land, width) in enumerate(plan):
            if row == j:
                made.append(pltpu.make_async_remote_copy(
                    src_ref=win.at[REACH + row, :, pl.ds(first * bs, width * bs)],
                    dst_ref=win.at[there, :, pl.ds(land * bs, width * bs)],
                    send_sem=send_sem.at[step, at],
                    recv_sem=recv_sem.at[step, at],
                    device_id=device(away),
                    device_id_type=pl.DeviceIdType.MESH,
                ))
        return made

    first_copies = []
    for j in range(rows):
        d = patt_gap[j]

        @pl.loop(0, BAND)
        def _(o):
            win1[REACH + j, :, cols(j + o)] = spread(cur_ref, j, o, d).astype(jnp.bfloat16)

        if j == 0:
            pl.semaphore_wait(barrier, len(peers))
        for copy in copies(win1, 0, j):
            copy.start()
            first_copies.append(copy)

    hd[...] = jnp.zeros_like(hd)
    for j in range(rows):
        d = coup_gap[j]

        @pl.loop(0, BAND)
        def _(o):
            hd[j * bs:(j + 1) * bs, cols(j + o)] = spread(h_ref, j, o, d).astype(jnp.bfloat16)

    for win in (win1, win2):
        for l in range(window):
            if l > REACH:
                n = l - REACH
                win[l, :, 0:n * bs] = jnp.zeros((bs, n * bs), jnp.bfloat16)
            if l + REACH + 1 < padded:
                n = padded - (l + REACH + 1)
                win[l, :, (l + REACH + 1) * bs:] = jnp.zeros((bs, n * bs), jnp.bfloat16)

    def multiply(win):
        @pl.loop(0, padded // 2)
        def _(t):
            right = win[:, :, cols(2 * t, 2)].reshape(window * bs, 2 * bs)
            acc[:, cols(2 * t, 2)] = jnp.dot(hd[...], right, preferred_element_type=jnp.float32)

    for copy in first_copies:
        copy.wait_recv()
    multiply(win1)

    second_copies = []
    for j in range(rows):
        d = patt_gap[j]

        @pl.loop(0, BAND)
        def _(o):
            keep = jnp.where(o == d, 0.0, 1.0)
            block = 2.0 * acc[j * bs:(j + 1) * bs, cols(j + o)] - spread(prev_ref, j, o, d)
            win2[REACH + j, :, cols(j + o)] = (block * keep).astype(jnp.bfloat16)

        for copy in copies(win2, 1, j):
            copy.start()
            second_copies.append(copy)

    for j in range(rows):
        d = patt_gap[j]

        @pl.loop(0, slots)
        def _(m):
            next_ref[j, m] = packed(win2, (REACH + j, slice(None)), j, m, d).astype(jnp.bfloat16)

    for copy in second_copies:
        copy.wait_recv()
    multiply(win2)

    for j in range(rows):
        d = patt_gap[j]

        @pl.loop(0, slots)
        def _(m):
            total = packed(acc, (slice(j * bs, (j + 1) * bs),), j, m, d)
            block = 2.0 * total - cur_ref[j, m].astype(jnp.float32)
            after_ref[j, m] = block.astype(jnp.bfloat16)

    for copy in first_copies + second_copies:
        copy.wait_send()


def body(count, hamiltonian, coupling_cols, pattern_cols, current_term, previous_term):
    rows, slots, bs, _ = current_term.shape
    window = rows + 2 * REACH
    padded = window + window % 2
    made = len(exchanges(rows))
    vmem = pl.BlockSpec(memory_space=pltpu.VMEM)
    smem = pl.BlockSpec(memory_space=pltpu.SMEM)
    term = jax.ShapeDtypeStruct(current_term.shape, jnp.bfloat16)
    return pl.pallas_call(
        functools.partial(kernel, count),
        out_shape=(term, term),
        in_specs=[vmem, smem, smem, vmem, vmem],
        out_specs=(vmem, vmem),
        scratch_shapes=[
            pltpu.VMEM((rows * bs, window * bs), jnp.bfloat16),
            pltpu.VMEM((rows * bs, padded * bs), jnp.float32),
            pltpu.VMEM((window, bs, padded * bs), jnp.bfloat16),
            pltpu.VMEM((window, bs, padded * bs), jnp.bfloat16),
            pltpu.SemaphoreType.DMA((2, made)),
            pltpu.SemaphoreType.DMA((2, made)),
        ],
        compiler_params=pltpu.CompilerParams(
            collective_id=0, has_side_effects=True, vmem_limit_bytes=52 * 2**20
        ),
    )(hamiltonian, coupling_cols, pattern_cols, current_term, previous_term)


def solution(mesh):
    split = P(("groups", "row"), None, None, None)
    placed = (split, P(("groups", "row"), None), P(("groups", "row"), None), split, split)
    return jax.shard_map(
        functools.partial(body, mesh.shape["row"]),
        mesh=mesh,
        in_specs=placed,
        out_specs=(split, split),
        check_vma=False,
    )
```

time: 632 us -> 220 us (0.35)
  waiting for transfers between devices: 286 us -> 0 us
  Pallas kernels: 0 us -> 215 us
  local copies, waits for them, and re-layouts: 161 us -> 4.47 us
  matrix products: 108 us -> 0 us
  other arithmetic: 46.8 us -> 0 us
  starting transfers between devices: 25.7 us -> 0 us
    ppermute x18 -> x0, waiting for transfers between devices: 286 us -> none  [passed_along(): return lax.ppermute(value, axis, pairs)]
    pallas_call x0 -> x1, Pallas kernels: none -> 215 us  [body(): pl.pallas_call(functools.partial(kernel, count), out_shape=(term, term),...]
    dot_general x12 -> x0, matrix products: 108 us -> none  [the longest x6 73.3 us: advance_row(): jnp.einsum('kmn,knab->kmab', matches, picked, preferred_element_type=jnp....]
    dot_general x6 -> x0, local copies, waits for them, and re-layouts: 74.8 us -> none  [advance_row(): jnp.einsum('kmn,knab->kmab', matches, picked, preferred_element_type=jnp....]
    gather x12 -> x0, local copies, waits for them, and re-layouts: 55.7 us -> none  [the longest x6 52.3 us: advance_row(): picked = jnp.take(values, neighbours, axis=0)]
    select_n x13 -> x0, other arithmetic: 46.7 us -> none  [the longest x6 45.5 us: advance_row(): picked = jnp.take(values, neighbours, axis=0)]
    ppermute x18 -> x0, starting transfers between devices: 25.7 us -> none  [passed_along(): return lax.ppermute(value, axis, pairs)]
    unnamed x24 -> x8, local copies, waits for them, and re-layouts: 17.5 us -> 4.47 us
  transfers between devices with their start and end apart: 18 -> 0, of which waited for: 11 -> 0; matrix products, arithmetic and copies ran while one was open for 2% -> 0% of each run, Pallas kernels for 0% -> 0%
where the time goes in v1:
time: 220 us
  Pallas kernels  215 us (98%)
  local copies, waits for them, and re-layouts  4.47 us (2%)
    pallas_call x1, Pallas kernels, body(): pl.pallas_call(functools.partial(kernel, count), out_shape=(term, term),...  215 us
    unnamed x8, local copies, waits for them, and re-layouts  4.47 us

profile of v1, /device:TPU:0, one launch (start us, length us, event | category | flops | bytes accessed | tf_op | source)
XLA Modules:
  0.0 219.7 jit_solution(7044310087808579519)
XLA Ops:
  0.6 0.0 copy-start
  0.6 0.7 copy-done
  1.3 0.0 copy-start.1
  1.3 0.7 copy-done.1
  2.0 214.6 %shard_map.68 = (bf16[3,16,128,128]{3,2,1,0:T(8,128)(2,1)S(1)}, bf16[3,16,128,128]{3,2,1,0:T(8,128)(2,1)}) custom-call(bf16[3,16,128,128]{3,2,1,0:T(8,128)(2,1)} %h_ref.1, s32[3,16]{1,0:T(4,128)S(1)} %copy-done, s32[3,16]{1,0:T(4,128)S(1)} %copy-done.1, bf16[3,16,128,128]{3,2,1,0:T(8,128)(2,1)} %cur_ref.1, bf16[3,16,128,128]{3,2,1,0:T(8,128)(2,1)} %prev_ref.1), custom_call_target="tpu_custom_call" | custom-call | tf_op jit(solution)/shard_map/pallas_call | solution.py:173
  216.6 0.0 copy-start.2
  216.6 1.1 copy.9
  217.8 0.8 copy-done.2
  218.6 1.1 copy.10
Async XLA Ops:
  0.6 0.7 copy-start
  1.3 0.7 copy-start.1
  216.6 2.0 copy-start.2

commit v2 on v1

--- a/solution.py
+++ b/solution.py
@@ -27,7 +27,7 @@
 
 
 def kernel(count, h_ref, coup_ref, patt_ref, cur_ref, prev_ref, next_ref, after_ref,
-           hd, acc, win1, win2, send_sem, recv_sem):
+           hd, acc, win1, win2, send_sem, forward_sem, recv_sem):
     rows, slots, bs, _ = cur_ref.shape
     order = rows * count
     window = rows + 2 * REACH
@@ -69,21 +69,74 @@
     patt_gap = [gap(patt_ref, j) for j in range(rows)]
     coup_gap = [gap(coup_ref, j) for j in range(rows)]
 
-    def copies(win, step, j):
+    even = lax.rem(me, 2) == 0
+    direct = {0: (2, -1, -3, 1), 1: (-2, 1, 3, -1)}
+    handed = {0: {1: 2, 2: 3}, 1: {-1: -2, -2: -3}}
+    at_of = {entry[:2]: at for at, entry in enumerate(plan)}
+
+    def remote(win, step, src, at, sent, away):
+        _, _, there, _, land, width = plan[at]
+        return pltpu.make_async_remote_copy(
+            src_ref=win.at[src[0], :, pl.ds(src[1] * bs, width * bs)],
+            dst_ref=win.at[there, :, pl.ds(land * bs, width * bs)],
+            send_sem=sent.at[step, at],
+            recv_sem=recv_sem.at[step, at],
+            device_id=device(away),
+            device_id_type=pl.DeviceIdType.MESH,
+        )
+
+    def own(win, step, core, j):
+        keys = [(away, j) for away in direct[core] if (away, j) in at_of]
+        return [remote(win, step, (REACH + j, plan[at_of[key]][3]), at_of[key], send_sem, key[0])
+                for key in keys]
+
+    def passed(win, step, core):
+        side = 1 if core == 0 else -1
         made = []
-        for at, (away, row, there, first, land, width) in enumerate(plan):
-            if row == j:
-                made.append(pltpu.make_async_remote_copy(
-                    src_ref=win.at[REACH + row, :, pl.ds(first * bs, width * bs)],
-                    dst_ref=win.at[there, :, pl.ds(land * bs, width * bs)],
-                    send_sem=send_sem.at[step, at],
-                    recv_sem=recv_sem.at[step, at],
-                    device_id=device(away),
-                    device_id_type=pl.DeviceIdType.MESH,
-                ))
+        for j in range(rows):
+            for away, onward in handed[core].items():
+                if (onward, j) in at_of:
+                    at = at_of[onward, j]
+                    src = (plan[at][2] + side * rows, plan[at][4] + side * rows)
+                    made.append((at_of[away, j], remote(win, step, src, at, forward_sem, side)))
         return made
 
-    first_copies = []
+    def arrival(win, step, at):
+        return remote(win, step, (REACH, 0), at, send_sem, plan[at][0])
+
+    def on_core(core):
+        return pl.when(even if core == 0 else jnp.logical_not(even))
+
+    def start_rows(win, step, j):
+        for core in (0, 1):
+            @on_core(core)
+            def _(core=core):
+                for copy in own(win, step, core, j):
+                    copy.start()
+
+    def receive(win, step):
+        for core in (0, 1):
+            @on_core(core)
+            def _(core=core):
+                done = set()
+                for at, copy in passed(win, step, core):
+                    arrival(win, step, at).wait_recv()
+                    copy.start()
+                    done.add(at)
+                for at in range(len(plan)):
+                    if at not in done:
+                        arrival(win, step, at).wait_recv()
+
+    def finish(win, step):
+        for core in (0, 1):
+            @on_core(core)
+            def _(core=core):
+                for j in range(rows):
+                    for copy in own(win, step, core, j):
+                        copy.wait_send()
+                for _, copy in passed(win, step, core):
+                    copy.wait_send()
+
     for j in range(rows):
         d = patt_gap[j]
 
@@ -93,9 +146,7 @@
 
         if j == 0:
             pl.semaphore_wait(barrier, len(peers))
-        for copy in copies(win1, 0, j):
-            copy.start()
-            first_copies.append(copy)
+        start_rows(win1, 0, j)
 
     hd[...] = jnp.zeros_like(hd)
     for j in range(rows):
@@ -120,11 +171,9 @@
             right = win[:, :, cols(2 * t, 2)].reshape(window * bs, 2 * bs)
             acc[:, cols(2 * t, 2)] = jnp.dot(hd[...], right, preferred_element_type=jnp.float32)
 
-    for copy in first_copies:
-        copy.wait_recv()
+    receive(win1, 0)
     multiply(win1)
 
-    second_copies = []
     for j in range(rows):
         d = patt_gap[j]
 
@@ -134,9 +183,7 @@
             block = 2.0 * acc[j * bs:(j + 1) * bs, cols(j + o)] - spread(prev_ref, j, o, d)
             win2[REACH + j, :, cols(j + o)] = (block * keep).astype(jnp.bfloat16)
 
-        for copy in copies(win2, 1, j):
-            copy.start()
-            second_copies.append(copy)
+        start_rows(win2, 1, j)
 
     for j in range(rows):
         d = patt_gap[j]
@@ -145,8 +192,7 @@
         def _(m):
             next_ref[j, m] = packed(win2, (REACH + j, slice(None)), j, m, d).astype(jnp.bfloat16)
 
-    for copy in second_copies:
-        copy.wait_recv()
+    receive(win2, 1)
     multiply(win2)
 
     for j in range(rows):
@@ -158,8 +204,8 @@
             block = 2.0 * total - cur_ref[j, m].astype(jnp.float32)
             after_ref[j, m] = block.astype(jnp.bfloat16)
 
-    for copy in first_copies + second_copies:
-        copy.wait_send()
+    finish(win1, 0)
+    finish(win2, 1)
 
 
 def body(count, hamiltonian, coupling_cols, pattern_cols, current_term, previous_term):
@@ -182,6 +228,7 @@
             pltpu.VMEM((window, bs, padded * bs), jnp.bfloat16),
             pltpu.SemaphoreType.DMA((2, made)),
             pltpu.SemaphoreType.DMA((2, made)),
+            pltpu.SemaphoreType.DMA((2, made)),
         ],
         compiler_params=pltpu.CompilerParams(
             collective_id=0, has_side_effects=True, vmem_limit_bytes=52 * 2**20

time: 220 us -> 149 us (0.68)
  Pallas kernels: 215 us -> 143 us
    pallas_call x1, Pallas kernels: 215 us -> 143 us  [body(): pl.pallas_call(functools.partial(kernel, count), out_shape=(term, term),...]
where the time goes in v2:
time: 149 us; the launch traced here: 148 us
  Pallas kernels  143 us (96%)
  local copies, waits for them, and re-layouts  4.47 us (3%)
    pallas_call x1, Pallas kernels, body(): pl.pallas_call(functools.partial(kernel, count), out_shape=(term, term),...  143 us
    unnamed x8, local copies, waits for them, and re-layouts  4.47 us

profile of v2, /device:TPU:0, one launch (start us, length us, event | category | flops | bytes accessed | tf_op | source)
XLA Modules:
  0.0 148.4 jit_solution(4703382400900211841)
XLA Ops:
  0.6 0.0 copy-start
  0.6 0.7 copy-done
  1.3 0.0 copy-start.1
  1.3 0.7 copy-done.1
  2.0 143.3 %shard_map.68 = (bf16[3,16,128,128]{3,2,1,0:T(8,128)(2,1)S(1)}, bf16[3,16,128,128]{3,2,1,0:T(8,128)(2,1)}) custom-call(bf16[3,16,128,128]{3,2,1,0:T(8,128)(2,1)} %h_ref.1, s32[3,16]{1,0:T(4,128)S(1)} %copy-done, s32[3,16]{1,0:T(4,128)S(1)} %copy-done.1, bf16[3,16,128,128]{3,2,1,0:T(8,128)(2,1)} %cur_ref.1, bf16[3,16,128,128]{3,2,1,0:T(8,128)(2,1)} %prev_ref.1), custom_call_target="tpu_custom_call" | custom-call | tf_op jit(solution)/shard_map/pallas_call | solution.py:219
  145.3 0.0 copy-start.2
  145.3 1.1 copy.9
  146.4 0.8 copy-done.2
  147.3 1.1 copy.10
Async XLA Ops:
  0.6 0.7 copy-start
  1.3 0.7 copy-start.1
  145.3 2.0 %copy-start.2 = (bf16[3,16,128,128]{3,2,1,0:T(8,128)(2,1)S(1)}, bf16[3,16,128,128]{3,2,1,0:T(8,128)(2,1)}, u32[]{:S(2)}) copy-start(bf16[3,16,128,128]{3,2,1,0:T(8,128)(2,1)} %get-tuple-element.5) | copy-start | bytes 4718596

commit v3 on v1

--- a/solution.py
+++ b/solution.py
@@ -27,7 +27,7 @@
 
 
 def kernel(count, h_ref, coup_ref, patt_ref, cur_ref, prev_ref, next_ref, after_ref,
-           hd, acc, win1, win2, send_sem, recv_sem):
+           hd, acc, win1, win2, send_sem, forward_sem, relay_sem, recv_sem):
     rows, slots, bs, _ = cur_ref.shape
     order = rows * count
     window = rows + 2 * REACH
@@ -69,21 +69,103 @@
     patt_gap = [gap(patt_ref, j) for j in range(rows)]
     coup_gap = [gap(coup_ref, j) for j in range(rows)]
 
-    def copies(win, step, j):
+    role = lax.rem(me, 4)
+    direct = {0: (2, -1, -3, 1), 1: (1, -2, 3, -1), 2: (-1, 2, -3, 1), 3: (-2, 1, 3, -1)}
+    handed = {0: {1: 2, 2: 3}, 1: {-1: -2, -2: -3}}
+    relayed = {0: {}, 1: {-1: 2, -2: 1}, 2: {1: -2, 2: -1}, 3: {}}
+    at_of = {entry[:2]: at for at, entry in enumerate(plan)}
+    shared = BAND - 1 - 2 * rows
+
+    def parts(at, core):
+        away, width = plan[at][0], plan[at][5]
+        if core == 0 and away in (1, 2):
+            return ((0, shared), (shared, width - shared))
+        if core == 1 and away in (-1, -2):
+            return ((width - shared, shared), (0, width - shared))
+        return ((0, width),)
+
+    def remote(win, step, at, part, core, row, shift, sent, away):
+        _, _, there, _, land, _ = plan[at]
+        first, width = parts(at, core)[part]
+        first = first + land
+        return pltpu.make_async_remote_copy(
+            src_ref=win.at[row, :, pl.ds((first + shift) * bs, width * bs)],
+            dst_ref=win.at[there, :, pl.ds(first * bs, width * bs)],
+            send_sem=sent.at[step, at, part],
+            recv_sem=recv_sem.at[step, at, part],
+            device_id=device(away),
+            device_id_type=pl.DeviceIdType.MESH,
+        )
+
+    def own(win, step, part_role, j):
         made = []
-        for at, (away, row, there, first, land, width) in enumerate(plan):
-            if row == j:
-                made.append(pltpu.make_async_remote_copy(
-                    src_ref=win.at[REACH + row, :, pl.ds(first * bs, width * bs)],
-                    dst_ref=win.at[there, :, pl.ds(land * bs, width * bs)],
-                    send_sem=send_sem.at[step, at],
-                    recv_sem=recv_sem.at[step, at],
-                    device_id=device(away),
-                    device_id_type=pl.DeviceIdType.MESH,
-                ))
+        for away in direct[part_role]:
+            if (away, j) in at_of:
+                at = at_of[away, j]
+                core = (part_role + away) % 2
+                split = len(parts(at, core)) == 2
+                for part in range(2 if split else 1):
+                    if split and part == 0 and (away > 0) == (part_role >= 2):
+                        continue
+                    made.append(remote(win, step, at, part, core, REACH + j, away * rows,
+                                       send_sem, away))
         return made
 
-    first_copies = []
+    def onward(win, step, at, part, core, side, sent):
+        return remote(win, step, at, part, core, plan[at][2] + side * rows, side * rows, sent, side)
+
+    def arrival(win, step, at, part, core):
+        first = plan[at][4] + parts(at, core)[part][0]
+        return remote(win, step, at, part, core, REACH, -first, send_sem, plan[at][0])
+
+    def receive(win, step, part_role):
+        core = part_role % 2
+        made = []
+        done = set()
+        for j in range(rows):
+            for away, further in handed[core].items():
+                at = at_of[away, j]
+                done.add(at)
+                arrival(win, step, at, 0, core).wait_recv()
+                if away in relayed[part_role]:
+                    copy = onward(win, step, at_of[relayed[part_role][away], j], 0, 1 - core,
+                                  3 if core else -3, relay_sem)
+                    copy.start()
+                    made.append(copy)
+                arrival(win, step, at, 1, core).wait_recv()
+                if (further, j) in at_of:
+                    copy = onward(win, step, at_of[further, j], 0, 1 - core,
+                                  -1 if core else 1, forward_sem)
+                    copy.start()
+                    made.append(copy)
+        for at in range(len(plan)):
+            if at not in done:
+                arrival(win, step, at, 0, core).wait_recv()
+        return made
+
+    def by_role(act):
+        for part_role in range(4):
+            @pl.when(role == part_role)
+            def _(part_role=part_role):
+                act(part_role)
+
+    def start_rows(win, step, j):
+        def act(part_role):
+            for copy in own(win, step, part_role, j):
+                copy.start()
+
+        by_role(act)
+
+    def receive_all(win, step):
+        def act(part_role):
+            for copy in receive(win, step, part_role):
+                copy.wait_send()
+            for j in range(rows):
+                for copy in own(win, step, part_role, j):
+                    copy.wait_send()
+
+        by_role(act)
+
     for j in range(rows):
         d = patt_gap[j]
 
@@ -93,9 +175,7 @@
 
         if j == 0:
             pl.semaphore_wait(barrier, len(peers))
-        for copy in copies(win1, 0, j):
-            copy.start()
-            first_copies.append(copy)
+        start_rows(win1, 0, j)
 
     hd[...] = jnp.zeros_like(hd)
     for j in range(rows):
@@ -120,11 +200,9 @@
             right = win[:, :, cols(2 * t, 2)].reshape(window * bs, 2 * bs)
             acc[:, cols(2 * t, 2)] = jnp.dot(hd[...], right, preferred_element_type=jnp.float32)
 
-    for copy in first_copies:
-        copy.wait_recv()
+    receive_all(win1, 0)
     multiply(win1)
 
-    second_copies = []
     for j in range(rows):
         d = patt_gap[j]
 
@@ -134,9 +212,7 @@
             block = 2.0 * acc[j * bs:(j + 1) * bs, cols(j + o)] - spread(prev_ref, j, o, d)
             win2[REACH + j, :, cols(j + o)] = (block * keep).astype(jnp.bfloat16)
 
-        for copy in copies(win2, 1, j):
-            copy.start()
-            second_copies.append(copy)
+        start_rows(win2, 1, j)
 
     for j in range(rows):
         d = patt_gap[j]
@@ -145,8 +221,7 @@
         def _(m):
             next_ref[j, m] = packed(win2, (REACH + j, slice(None)), j, m, d).astype(jnp.bfloat16)
 
-    for copy in second_copies:
-        copy.wait_recv()
+    receive_all(win2, 1)
     multiply(win2)
 
     for j in range(rows):
@@ -157,9 +232,6 @@
             total = packed(acc, (slice(j * bs, (j + 1) * bs),), j, m, d)
             block = 2.0 * total - cur_ref[j, m].astype(jnp.float32)
             after_ref[j, m] = block.astype(jnp.bfloat16)
-
-    for copy in first_copies + second_copies:
-        copy.wait_send()
 
 
 def body(count, hamiltonian, coupling_cols, pattern_cols, current_term, previous_term):
@@ -180,8 +252,10 @@
             pltpu.VMEM((rows * bs, padded * bs), jnp.float32),
             pltpu.VMEM((window, bs, padded * bs), jnp.bfloat16),
             pltpu.VMEM((window, bs, padded * bs), jnp.bfloat16),
-            pltpu.SemaphoreType.DMA((2, made)),
-            pltpu.SemaphoreType.DMA((2, made)),
+            pltpu.SemaphoreType.DMA((2, made, 2)),
+            pltpu.SemaphoreType.DMA((2, made, 2)),
+            pltpu.SemaphoreType.DMA((2, made, 2)),
+            pltpu.SemaphoreType.DMA((2, made, 2)),
         ],
         compiler_params=pltpu.CompilerParams(
             collective_id=0, has_side_effects=True, vmem_limit_bytes=52 * 2**20

time: 220 us -> 126 us (0.57)
  Pallas kernels: 215 us -> 121 us
    pallas_call x1, Pallas kernels: 215 us -> 121 us  [body(): pl.pallas_call(functools.partial(kernel, count), out_shape=(term, term),...]
where the time goes in v3:
time: 126 us
  Pallas kernels  121 us (96%)
  local copies, waits for them, and re-layouts  4.47 us (4%)
    pallas_call x1, Pallas kernels, body(): pl.pallas_call(functools.partial(kernel, count), out_shape=(term, term),...  121 us
    unnamed x8, local copies, waits for them, and re-layouts  4.47 us

profile of v3, /device:TPU:0, one launch (start us, length us, event | category | flops | bytes accessed | tf_op | source)
XLA Modules:
  0.0 125.9 jit_solution(18340369802547880837)
XLA Ops:
  0.6 0.0 copy-start
  0.6 0.7 copy-done
  1.3 0.0 copy-start.1
  1.3 0.7 copy-done.1
  2.0 120.8 %shard_map.68 = (bf16[3,16,128,128]{3,2,1,0:T(8,128)(2,1)S(1)}, bf16[3,16,128,128]{3,2,1,0:T(8,128)(2,1)}) custom-call(bf16[3,16,128,128]{3,2,1,0:T(8,128)(2,1)} %h_ref.1, s32[3,16]{1,0:T(4,128)S(1)} %copy-done, s32[3,16]{1,0:T(4,128)S(1)} %copy-done.1, bf16[3,16,128,128]{3,2,1,0:T(8,128)(2,1)} %cur_ref.1, bf16[3,16,128,128]{3,2,1,0:T(8,128)(2,1)} %prev_ref.1), custom_call_target="tpu_custom_call" | custom-call | tf_op jit(solution)/shard_map/pallas_call | solution.py:245
  122.8 0.0 copy-start.2
  122.8 1.1 copy.9
  123.9 0.8 copy-done.2
  124.7 1.1 copy.10
Async XLA Ops:
  0.6 0.7 copy-start
  1.3 0.7 copy-start.1
  122.8 2.0 %copy-start.2 = (bf16[3,16,128,128]{3,2,1,0:T(8,128)(2,1)S(1)}, bf16[3,16,128,128]{3,2,1,0:T(8,128)(2,1)}, u32[]{:S(2)}) copy-start(bf16[3,16,128,128]{3,2,1,0:T(8,128)(2,1)} %get-tuple-element.5) | copy-start | bytes 4718596

commit v4 on v3

--- a/solution.py
+++ b/solution.py
@@ -195,10 +195,11 @@
                 win[l, :, (l + REACH + 1) * bs:] = jnp.zeros((bs, n * bs), jnp.bfloat16)
 
     def multiply(win):
-        @pl.loop(0, padded // 2)
-        def _(t):
-            right = win[:, :, cols(2 * t, 2)].reshape(window * bs, 2 * bs)
-            acc[:, cols(2 * t, 2)] = jnp.dot(hd[...], right, preferred_element_type=jnp.float32)
+        for c in range(0, padded, 2):
+            low, high = max(0, c - REACH), min(window, c + REACH + 2)
+            right = win[low:high, :, c * bs:(c + 2) * bs].reshape((high - low) * bs, 2 * bs)
+            left = hd[:, low * bs:high * bs]
+            acc[:, c * bs:(c + 2) * bs] = jnp.dot(left, right, preferred_element_type=jnp.float32)
 
     receive_all(win1, 0)
     multiply(win1)

time: 126 us -> 120 us (0.952)
  Pallas kernels: 121 us -> 115 us
    pallas_call x1, Pallas kernels: 121 us -> 115 us  [body(): pl.pallas_call(functools.partial(kernel, count), out_shape=(term, term),...]
where the time goes in v4:
time: 120 us
  Pallas kernels  115 us (96%)
  local copies, waits for them, and re-layouts  4.47 us (4%)
    pallas_call x1, Pallas kernels, body(): pl.pallas_call(functools.partial(kernel, count), out_shape=(term, term),...  115 us
    unnamed x8, local copies, waits for them, and re-layouts  4.47 us

profile of v4, /device:TPU:0, one launch (start us, length us, event | category | flops | bytes accessed | tf_op | source)
XLA Modules:
  0.0 119.7 jit_solution(117034438336467914)
XLA Ops:
  0.6 0.0 copy-start
  0.6 0.7 copy-done
  1.3 0.0 copy-start.1
  1.3 0.7 copy-done.1
  2.0 114.6 %shard_map.68 = (bf16[3,16,128,128]{3,2,1,0:T(8,128)(2,1)S(1)}, bf16[3,16,128,128]{3,2,1,0:T(8,128)(2,1)}) custom-call(bf16[3,16,128,128]{3,2,1,0:T(8,128)(2,1)} %h_ref.1, s32[3,16]{1,0:T(4,128)S(1)} %copy-done, s32[3,16]{1,0:T(4,128)S(1)} %copy-done.1, bf16[3,16,128,128]{3,2,1,0:T(8,128)(2,1)} %cur_ref.1, bf16[3,16,128,128]{3,2,1,0:T(8,128)(2,1)} %prev_ref.1), custom_call_target="tpu_custom_call" | custom-call | tf_op jit(solution)/shard_map/pallas_call | solution.py:246
  116.6 0.0 copy-start.2
  116.6 1.1 copy.9
  117.7 0.8 copy-done.2
  118.5 1.1 copy.10
Async XLA Ops:
  0.6 0.7 copy-start
  1.3 0.7 copy-start.1
  116.6 2.0 %copy-start.2 = (bf16[3,16,128,128]{3,2,1,0:T(8,128)(2,1)S(1)}, bf16[3,16,128,128]{3,2,1,0:T(8,128)(2,1)}, u32[]{:S(2)}) copy-start(bf16[3,16,128,128]{3,2,1,0:T(8,128)(2,1)} %get-tuple-element.5) | copy-start | bytes 4718596
